TPU v7x, 32 devices: a whole 2x2x4 slice. The times are simulated.
32 devices in a mesh: dp: 8 (over y, x, core), ctx: 4 (over z).
Axes of the slice: x: 2, y: 2, z: 4, core: 2. Of those that a mesh axis runs over, the one named last changes fastest.
Arguments:
- stream: bfloat16 [8, 512, 3072], P('dp', 'ctx'), may hold values from -210 to 210
- mod_shift: bfloat16 [8, 3072], P('dp'), may hold values from -3 to 3
- mod_scale: bfloat16 [8, 3072], P('dp'), may hold values from -1.796875 to 1.796875
- qkv_weight: bfloat16 [3072, 6144], P(None, 'dp'), may hold values from -0.109375 to 0.109375
- q_gain: float32 [128], replicated, may hold values from 0.7 to 2.2
- k_gain: float32 [128], replicated, may hold values from 0.7 to 2.2
Outputs:
- attended: bfloat16 [8, 512, 2048], P('dp', 'ctx')
All inputs are finite; a program needn't handle non-finite values.
Results may differ from a plain program's by a relative error of at most 0.0049.
Values may be sent and summed in bfloat16 or wider, within the bound.
A program may use at most 128 MiB of HBM per device.

v0:
```python
import math

import jax
import jax.numpy as jnp
from jax import lax
from jax.sharding import PartitionSpec as P

HD = 128
HEADS = 16
HW = 2048


def modulated_norm(hidden, shift, scale):
    embedded = hidden.astype(jnp.float32)
    mean = jnp.mean(embedded, axis=-1, keepdims=True)
    centred = embedded - mean
    var = jnp.mean(centred * centred, axis=-1, keepdims=True)
    return (
        centred * lax.rsqrt(var + 1e-06) * (1.0 + scale.astype(jnp.float32))
        + shift.astype(jnp.float32)
    ).astype(jnp.bfloat16)


def head_norm(values, gain):
    shaped = values.astype(jnp.float32).reshape(values.shape[0], HEADS, HD)
    scale = lax.rsqrt(jnp.mean(shaped * shaped, axis=-1, keepdims=True) + 1e-06)
    return (shaped * scale * gain).astype(jnp.bfloat16)


def shards(stream, mod_shift, mod_scale, qkv_weight, q_gain, k_gain):
    tok_rows = stream.shape[1]
    root_size = math.sqrt(HD)
    normed = modulated_norm(stream[0], mod_shift, mod_scale)
    flat = jnp.dot(
        lax.all_gather(normed, "dp", axis=0, tiled=True),
        qkv_weight,
        preferred_element_type=jnp.float32,
    ).astype(jnp.bfloat16)
    projected = flat.reshape(-1, tok_rows, flat.shape[-1])
    mine = lax.all_to_all(projected, "dp", split_axis=0, concat_axis=2, tiled=True)[0]
    qnorm = head_norm(mine[:, :HW], q_gain)
    knorm = head_norm(mine[:, HW : 2 * HW], k_gain)
    values = mine[:, 2 * HW :].reshape(tok_rows, HEADS, HD)
    key_rows = lax.all_gather(knorm, "ctx", axis=0, tiled=True)
    value_rows = lax.all_gather(values, "ctx", axis=0, tiled=True)
    scores = (
        jnp.einsum("qhd,khd->hqk", qnorm, key_rows, preferred_element_type=jnp.float32) / root_size
    )
    weights = jnp.exp(scores)
    totals = jnp.sum(weights, axis=-1)
    summed = jnp.einsum(
        "hqk,khd->hqd", weights.astype(jnp.bfloat16), value_rows, preferred_element_type=jnp.float32
    )
    summed, totals = (summed, totals)
    result = summed / totals[:, :, None]
    return jnp.transpose(result, (1, 0, 2)).reshape(1, tok_rows, HW).astype(jnp.bfloat16)


def solution(mesh):
    placed = (P("dp", "ctx", None), P("dp", None), P("dp", None), P(None, "dp"), P(), P())
    return jax.shard_map(
        shards, mesh=mesh, in_specs=placed, out_specs=P("dp", "ctx", None), check_vma=False
    )
```

profile of v0, /device:TPU:0, one launch (start us, length us, event | category | flops | bytes accessed | tf_op | source)
XLA Modules:
  0.0 199.4 jit_solution(6181851771061830574)
XLA Ops:
  6.5 0.0 copy-start
  6.5 0.0 all-gather.4.cloned.1.call-start
  6.5 1.4 convert_reduce_fusion
  7.9 1.5 fusion.8
  9.4 0.7 convert_add_fusion
  10.2 0.7 add.56
  10.9 0.0 copy-done
  10.9 1.3 fusion.11
  12.2 0.0 all-gather.4.cloned.1.call-update
  12.2 0.0 all-gather.6.cloned.1.call-start
  12.3 48.3 %all-gather.4.cloned.1.call-done = bf16[1024,3072]{1,0:T(8,128)(2,1)} async-done(((bf16[128,3072]{1,0:T(8,128)(2,1)}), bf16[1024,3072]{1,0:T(8,128)(2,1)}) %all-gather.4.cloned.1.call-update) | async-done | bytes 6291472 | tf_op jit(solution)/shard_map/all_gather | solution.py:35
  60.6 8.5 %convolution_convert_fusion = bf16[1024,768]{1,0:T(8,128)(2,1)S(1)} fusion(bf16[1024,3072]{1,0:T(8,128)(2,1)} %all-gather.4.cloned.1.call-done, bf16[3072,768]{1,0:T(8,128)(2,1)} %param.9), kind=kOutput, calls=%fused_computation.7 | convolution fusion | flops 4832624640 | bytes 12582912 | tf_op jit(solution)/shard_map/dot_general | solution.py:34
  69.1 0.9 copy.8
  70.0 23.5 %all_to_all.15 = bf16[8,128,768]{1,2,0:T(8,128)(2,1)S(1)} all-to-all(bf16[8,128,768]{1,2,0:T(8,128)(2,1)S(1)} %copy.8), channel_id=1, replica_groups=mesh['dp'=8,'ctx'=4] {'dp'}, dimensions={0} | all-to-all | bytes 3145728 | tf_op jit(solution)/shard_map/all_to_all | solution.py:40
  93.5 0.9 fusion.29
  94.4 0.0 copy-start.1
  94.4 0.2 fusion.21
  94.7 0.0 copy-start.2
  94.7 0.2 copy.9
  94.9 0.2 copy-done.1
  95.1 1.1 multiply_convert_fusion
  96.2 0.0 all-gather.6.cloned.1.call-update
  96.2 0.0 all-gather.8.cloned.1.call-start
  96.3 0.7 all-gather.8.cloned.1.call-update
  97.0 44.4 %all-gather.6.cloned.1.call-done = bf16[512,16,128]{2,0,1:T(8,128)(2,1)} async-done(((bf16[128,16,128]{2,0,1:T(8,128)(2,1)}), bf16[512,16,128]{2,0,1:T(8,128)(2,1)}) %all-gather.6.cloned.1.call-update) | async-done | bytes 2097168 | tf_op jit(solution)/shard_map/all_gather | solution.py:44
  141.4 0.0 copy-done.2
  141.4 4.5 %fusion = (f32[16,128]{1,0:T(8,128)S(1)}, f32[16,128,512]{2,1,0:T(8,128)}) fusion(bf16[512,16,128]{2,0,1:T(8,128)(2,1)} %all-gather.6.cloned.1.call-done, bf16[128,16,128]{0,2,1:T(8,128)(2,1)S(1)} %bitcast.47, f32[128]{0:T(128)S(1)} %copy-done.2, f32[128,16]{0,1:T(8,128)S(1)} %add_rsqrt_fusion.1), kind=kOutput, calls=%fused_computation.1 | convolution fusion | flops 271579136 | bytes 6832640 | tf_op jit(solution)/shard_map/qhd,khd->hqk/dot_general | solution.py:47
  145.9 42.1 %all-gather.8.cloned.1.call-done = bf16[512,16,128]{0,2,1:T(8,128)(2,1)} async-done(((bf16[128,16,128]{0,2,1:T(8,128)(2,1)}), bf16[512,16,128]{0,2,1:T(8,128)(2,1)}) %all-gather.8.cloned.1.call-update) | async-done | bytes 2097168 | tf_op jit(solution)/shard_map/all_gather | solution.py:45
  188.0 3.9 %fusion.18 = bf16[128,16,128]{0,2,1:T(8,128)(2,1)S(1)} fusion(bf16[512,16,128]{0,2,1:T(8,128)(2,1)} %all-gather.8.cloned.1.call-done, f32[16,128,512]{2,1,0:T(8,128)} %get-tuple-element.11, f32[128,16]{0,1:T(8,128)S(1)} %bitcast.52), kind=kOutput, calls=%fused_computation.19 | convolution fusion | flops 271056896 | bytes 6823936 | tf_op jit(solution)/shard_map/hqk,khd->hqd/dot_general | solution.py:51
  191.8 1.0 copy.11
  (4 shorter events, 0.0 us)
Async XLA Ops:
  6.5 4.4 %copy-start = (bf16[1,128,3072]{2,1,0:T(8,128)(2,1)S(1)}, bf16[1,128,3072]{2,1,0:T(8,128)(2,1)}, u32[]{:S(2)}) copy-start(bf16[1,128,3072]{2,1,0:T(8,128)(2,1)} %param.6) | copy-start | bytes 2359300
  6.5 54.0 %all-gather.4.cloned.1.call-start = ((), (), s32[]{:S(2)}) async-start(), calls=%async_computation.1 | async-start | bytes 7077888 | tf_op jit(solution)/shard_map/all_gather | solution.py:35
  12.2 129.2 %all-gather.6.cloned.1.call-start = ((), (), s32[]{:S(2)}) async-start(), calls=%async_computation.2 | async-start | bytes 2621440 | tf_op jit(solution)/shard_map/all_gather | solution.py:44
  94.4 0.7 copy-start.1
  94.7 46.7 %copy-start.2 = (f32[128]{0:T(128)S(1)}, f32[128]{0:T(128)}, u32[]{:S(2)}) copy-start(f32[128]{0:T(128)} %param.10) | copy-start | bytes 1540
  96.2 91.7 %all-gather.8.cloned.1.call-start = ((), (), s32[]{:S(2)}) async-start(), calls=%async_computation.3 | async-start | bytes 2621440 | tf_op jit(solution)/shard_map/all_gather | solution.py:45
Sparse Core Ops, SparseCore 0:
  12.3 48.2 all-gather.3
  96.4 44.9 all-gather.5
  143.0 44.9 all-gather.7
where the time goes:
time: 200 us; the launch traced here: 199 us
  waiting for transfers between devices  136 us (68%)
  blocking collectives  23.5 us (12%)
  matrix products  16.9 us (8%)
  between operations  13.2 us (7%)
  other arithmetic  6.99 us (3%)
  local copies, waits for them, and re-layouts  3.2 us (2%)
    all_gather x1, waiting for transfers between devices, shards(): lax.all_gather(normed, 'dp', axis=0, tiled=True)  48.3 us
    all_gather x1, waiting for transfers between devices, shards(): key_rows = lax.all_gather(knorm, 'ctx', axis=0, tiled=True)  44.4 us
    all_gather x1, waiting for transfers between devices, shards(): value_rows = lax.all_gather(values, 'ctx', axis=0, tiled=True)  42.1 us
    all_to_all x1, blocking collectives, shards(): lax.all_to_all(projected, 'dp', split_axis=0, concat_axis=2, tiled=True)[0]  23.5 us
    dot_general x1, matrix products, shards(): jnp.dot(lax.all_gather(normed, 'dp', axis=0, tiled=True), qkv_weight, pre...  8.52 us
    dot_general x1, matrix products, shards(): jnp.einsum('qhd,khd->hqk', qnorm, key_rows, preferred_element_type=jnp.fl...  4.49 us
  transfers between devices with their start and end apart: 3, of which 3 were waited for; matrix products, arithmetic and copies ran while one was open for 2% of the time, Pallas kernels for 0%

commit v1 on v0

v1 whole, which is shorter than its diff:
```python
import functools
import math

import jax
import jax.numpy as jnp
from jax import lax
from jax.experimental import pallas as pl
from jax.experimental.pallas import tpu as pltpu
from jax.sharding import PartitionSpec as P

HD = 128
HEADS = 16
HW = 2048
MESH = pl.DeviceIdType.MESH


def flip(index, mask):
    out = index
    bit = 1
    while bit <= mask:
        if mask & bit:
            out = out + bit - 2 * bit * ((index // bit) % 2)
        bit *= 2
    return out


def last_hop(role, half):
    if half == 0:
        return role.bit_length() - 1
    return (role & -role).bit_length() - 1


def kernel(
    dp, ctx, unit,
    stream_ref, shift_ref, scale_ref, weight_hbm, qg_ref, kg_ref,
    out_ref,
    toks, weight, proj, mine, heads, outs,
    w_sem, t_send, t_recv, p_send, m_recv, z_send, r_sem, o_send, o_recv,
):
    i = lax.axis_index("dp")
    z = lax.axis_index("ctx")
    rows = stream_ref.shape[1]
    chips = dp // 2
    bits = chips.bit_length() - 1
    half_rows = rows // 2
    cols = weight.shape[1]
    m = cols // unit
    width = HW // ctx
    sub = width // unit
    seq = rows * ctx

    load = pltpu.make_async_copy(weight_hbm, weight, w_sem)
    load.start()

    barrier = pltpu.get_barrier_semaphore()
    for q in range(1, dp):
        pl.semaphore_signal(barrier, inc=1, device_id={"dp": flip(i, q)}, device_id_type=MESH)
    for k in range(1, ctx):
        pl.semaphore_signal(
            barrier, inc=1, device_id={"ctx": lax.rem(z + k, ctx)}, device_id_type=MESH
        )

    gain = 1.0 + scale_ref[...].astype(jnp.float32)
    shift = shift_ref[...].astype(jnp.float32)

    def norm_rows(at, _):
        hid = stream_ref[0, pl.ds(at * 16, 16), :].astype(jnp.float32)
        mean = jnp.mean(hid, axis=-1, keepdims=True)
        cen = hid - mean
        var = jnp.mean(cen * cen, axis=-1, keepdims=True)
        toks[0, pl.ds(at * 16, 16), :] = (cen * lax.rsqrt(var + 1e-06) * gain + shift).astype(
            jnp.bfloat16
        )
        return 0

    t_sent = []

    def send_tok(role_from, to_mask, role_to, sib, half):
        n = len(t_sent)
        copy = pltpu.make_async_remote_copy(
            src_ref=toks.at[role_from, pl.ds(half * half_rows, half_rows), :],
            dst_ref=toks.at[role_to, pl.ds(sib * rows + half * half_rows, half_rows), :],
            send_sem=t_send.at[n],
            recv_sem=t_recv.at[role_to, sib, half],
            device_id={"dp": flip(i, to_mask)},
            device_id_type=MESH,
        )
        copy.start()
        t_sent.append(copy)

    def wait_tok(role, sib, half):
        part = toks.at[role, pl.ds(sib * rows + half * half_rows, half_rows), :]
        pltpu.make_async_copy(part, part, t_recv.at[role, sib, half]).wait()

    def pass_on(role, half):
        for bit in range(bits):
            to = role ^ (1 << bit)
            if role >> bit & 1:
                continue
            if role == 0 or last_hop(to, half) == bit:
                send_tok(role, 2 << bit, to, 0, half)
        send_tok(role, 1, role, 1, half)

    steps = half_rows // 16
    lax.fori_loop(0, steps, norm_rows, 0)
    pl.semaphore_wait(barrier, dp + ctx - 2)
    pass_on(0, 0)
    lax.fori_loop(steps, 2 * steps, norm_rows, 0)
    pass_on(0, 1)

    qg = qg_ref[...]
    kg = kg_ref[...]
    p_sent = []

    def project(role):
        def one(j, _):
            u = m * i + j
            kind = u // (ctx * sub)
            flat = jnp.dot(
                toks[role],
                weight[:, pl.ds(pl.multiple_of(j * unit, unit), unit)],
                preferred_element_type=jnp.float32,
            ).astype(jnp.bfloat16)
            head_gain = jnp.where(kind == 0, qg, kg)
            for h in range(unit // HD):
                raw = flat[:, h * HD : (h + 1) * HD]
                val = raw.astype(jnp.float32)
                inv = lax.rsqrt(jnp.mean(val * val, axis=-1, keepdims=True) + 1e-06)
                res = jnp.where(kind < 2, val * inv * head_gain, val).astype(jnp.bfloat16)
                proj[2 * role, j, :, h * HD : (h + 1) * HD] = res[:rows]
                proj[2 * role + 1, j, :, h * HD : (h + 1) * HD] = res[rows:]
            return 0

        lax.fori_loop(0, m, one, 0)
        for k in range(2):
            q = 2 * role + k
            dst = mine.at[pl.ds(m * i, m)]
            if q == 0:
                copy = pltpu.make_async_copy(proj.at[0], dst, m_recv.at[i])
                copy.start()
            else:
                copy = pltpu.make_async_remote_copy(
                    src_ref=proj.at[q],
                    dst_ref=dst,
                    send_sem=p_send.at[q],
                    recv_sem=m_recv.at[i],
                    device_id={"dp": flip(i, q)},
                    device_id_type=MESH,
                )
                copy.start()
                p_sent.append(copy)

    def z_copy(q, j):
        u = m * flip(i, q) + j
        kind = u // (ctx * sub)
        to = (u // sub) % ctx
        h = u % sub
        src = mine.at[u]
        dst = heads.at[h, kind, pl.ds(z * rows, rows), :]

        def local():
            return pltpu.make_async_copy(src, dst, r_sem.at[h])

        def remote():
            return pltpu.make_async_remote_copy(
                src_ref=src,
                dst_ref=dst,
                send_sem=z_send.at[q * m + j],
                recv_sem=r_sem.at[h],
                device_id={"ctx": to},
                device_id_type=MESH,
            )

        return to, local, remote

    def to_heads(role):
        for q in (2 * role, 2 * role + 1):
            src = flip(i, q)
            part = mine.at[pl.ds(m * src, m)]
            pltpu.make_async_copy(part, part, m_recv.at[src]).wait()
            for j in range(m):
                to, local, remote = z_copy(q, j)
                pl.when(to == z)(lambda: local().start())
                pl.when(to != z)(lambda: remote().start())

    def wait_sib(role):
        for half in range(2):
            wait_tok(role, 1, half)

    load.wait()
    wait_sib(0)
    project(0)
    levels = [[r for r in range(chips) if r.bit_count() == n] for n in range(1, bits + 1)]
    done = [0]
    for level in levels:
        order = [(r, half) for half in range(2) for r in level]
        if len(level) == 2:
            order = [(level[0], 0), (level[1], 1), (level[0], 1), (level[1], 0)]
        for r, half in order:
            wait_tok(r, 0, half)
            pass_on(r, half)
        for r in done:
            to_heads(r)
        for r in level:
            wait_sib(r)
            project(r)
        done = level
    for r in done:
        to_heads(r)

    for h in range(sub):
        pltpu.make_async_copy(heads.at[h], heads.at[h], r_sem.at[h]).wait()

    root = 1.0 / math.sqrt(HD)
    o_sent = []
    for k in list(range(1, ctx)) + [0]:
        t = lax.rem(z + k, ctx)
        at = pl.ds(pl.multiple_of(t * rows, rows), rows)
        for h in range(sub):
            for p in range(unit // HD):
                lanes = slice(p * HD, (p + 1) * HD)
                scores = lax.dot_general(
                    heads[h, 0, at, lanes],
                    heads[h, 1, :, lanes],
                    (((1,), (1,)), ((), ())),
                    preferred_element_type=jnp.float32,
                )
                weights = jnp.exp(scores * root)
                totals = jnp.sum(weights, axis=-1, keepdims=True)
                summed = jnp.dot(
                    weights.astype(jnp.bfloat16),
                    heads[h, 2, :, lanes],
                    preferred_element_type=jnp.float32,
                )
                outs[k, :, pl.ds(h * unit + p * HD, HD)] = (summed / totals).astype(jnp.bfloat16)
        dst = out_ref.at[0, :, pl.ds(pl.multiple_of(z * width, width), width)]
        if k:
            copy = pltpu.make_async_remote_copy(
                src_ref=outs.at[k],
                dst_ref=dst,
                send_sem=o_send.at[k],
                recv_sem=o_recv.at[z],
                device_id={"ctx": t},
                device_id_type=MESH,
            )
            copy.start()
            o_sent.append(copy)
        else:
            pltpu.make_async_copy(outs.at[0], dst, o_recv.at[z]).start()

    for s in range(ctx):
        part = out_ref.at[0, :, pl.ds(s * width, width)]
        pltpu.make_async_copy(part, part, o_recv.at[s]).wait()
    for copy in t_sent + p_sent + o_sent:
        copy.wait_send()
    for q in range(dp):
        for j in range(m):
            to, _, remote = z_copy(q, j)
            pl.when(to != z)(lambda: remote().wait_send())


def shards(mesh, stream, mod_shift, mod_scale, qkv_weight, q_gain, k_gain):
    dp, ctx = mesh.shape["dp"], mesh.shape["ctx"]
    rows, depth = stream.shape[1:]
    cols = qkv_weight.shape[1]
    chips = dp // 2
    width = HW // ctx
    unit = math.gcd(cols, width)
    m = cols // unit
    sub = width // unit
    seq = rows * ctx
    dma = pltpu.SemaphoreType.DMA
    vmem = pl.BlockSpec(memory_space=pltpu.VMEM)
    return pl.pallas_call(
        functools.partial(kernel, dp, ctx, unit),
        out_shape=jax.ShapeDtypeStruct((1, rows, HW), jnp.bfloat16),
        in_specs=[vmem, vmem, vmem, pl.BlockSpec(memory_space=pl.ANY), vmem, vmem],
        out_specs=vmem,
        scratch_shapes=[
            pltpu.VMEM((chips, 2 * rows, depth), jnp.bfloat16),
            pltpu.VMEM((depth, cols), jnp.bfloat16),
            pltpu.VMEM((dp, m, rows, unit), jnp.bfloat16),
            pltpu.VMEM((dp * m, rows, unit), jnp.bfloat16),
            pltpu.VMEM((sub, 3, seq, unit), jnp.bfloat16),
            pltpu.VMEM((ctx, rows, width), jnp.bfloat16),
            dma,
            dma((4 * dp,)),
            dma((chips, 2, 2)),
            dma((dp,)),
            dma((dp,)),
            dma((dp * m,)),
            dma((sub,)),
            dma((ctx,)),
            dma((ctx,)),
        ],
        compiler_params=pltpu.CompilerParams(
            collective_id=0, has_side_effects=True, vmem_limit_bytes=56 * 1024 * 1024
        ),
    )(stream, mod_shift, mod_scale, qkv_weight, q_gain[None, :], k_gain[None, :])


def solution(mesh):
    placed = (P("dp", "ctx", None), P("dp", None), P("dp", None), P(None, "dp"), P(), P())
    return jax.shard_map(
        functools.partial(shards, mesh),
        mesh=mesh,
        in_specs=placed,
        out_specs=P("dp", "ctx", None),
        check_vma=False,
    )
```

time: 200 us -> 90.6 us (0.45)
  the two profiles are of different devices: /device:TPU:0 before, /device:TPU:30 now
where the time goes in v1:
time: 90.6 us; the launch traced here: 89.2 us
  Pallas kernels  87.3 us (96%)
  local copies, waits for them, and re-layouts  1.88 us (2%)
    pallas_call x1, Pallas kernels, shards(): pl.pallas_call(functools.partial(kernel, dp, ctx, unit), out_shape=jax.Sh...  87.3 us
    unnamed x1, local copies, waits for them, and re-layouts  1.88 us

profile of v1, /device:TPU:30, one launch (start us, length us, event | category | flops | bytes accessed | tf_op | source)
XLA Modules:
  0.0 89.2 jit_solution(8216518646550491401)
XLA Ops:
  0.0 87.3 %shard_map.64 = bf16[1,128,2048]{2,1,0:T(8,128)(2,1)} custom-call(bf16[1,128,3072]{2,1,0:T(8,128)(2,1)} %stream_ref.1, bf16[1,3072]{1,0:T(2,128)(2,1)} %shift_ref.1, bf16[1,3072]{1,0:T(2,128)(2,1)} %scale_ref.1, bf16[3072,768]{1,0:T(8,128)(2,1)} %weight_hbm.1, f32[1,128]{1,0:T(1,128)} %bitcast.2, f32[1,128]{1,0:T(1,128)} %bitcast.3), custom_call_target="tpu_custom_call" | custom-call | tf_op jit(solution)/shard_map/pallas_call | solution.py:274
  87.3 1.9 %copy.8 = bf16[1,128,2048]{2,1,0:T(8,128)(2,1)} copy(bf16[1,128,2048]{2,1,0:T(8,128)(2,1)} %shard_map.64) | data formatting | bytes 1048576

commit v2 on v1

v2 whole, which is shorter than its diff:
```python
import functools
import math

import jax
import jax.numpy as jnp
from jax import lax
from jax.experimental import pallas as pl
from jax.experimental.pallas import tpu as pltpu
from jax.sharding import PartitionSpec as P

HD = 128
HEADS = 16
HW = 2048
MESH = pl.DeviceIdType.MESH
CHUNKS = 2


def flip(index, mask):
    out = index
    bit = 1
    while bit <= mask:
        if mask & bit:
            out = out + bit - 2 * bit * ((index // bit) % 2)
        bit *= 2
    return out


def last_hop(role, half):
    if half == 0:
        return role.bit_length() - 1
    return (role & -role).bit_length() - 1


def kernel(
    dp, ctx, unit,
    stream_ref, shift_ref, scale_ref, weight_hbm, qg_ref, kg_ref,
    out_ref,
    toks, weight, proj, mine, heads, outs,
    w_sem, t_send, t_recv, p_send, m_recv, z_send, r_sem, o_send, o_recv,
):
    i = lax.axis_index("dp")
    z = lax.axis_index("ctx")
    rows = stream_ref.shape[1]
    chips = dp // 2
    bits = chips.bit_length() - 1
    part = rows // CHUNKS
    piece = part // 2
    cols = weight.shape[1]
    m = cols // unit
    width = HW // ctx
    sub = width // unit
    seq = rows * ctx

    load = pltpu.make_async_copy(weight_hbm, weight, w_sem)
    load.start()

    barrier = pltpu.get_barrier_semaphore()
    for q in range(1, dp):
        pl.semaphore_signal(barrier, inc=1, device_id={"dp": flip(i, q)}, device_id_type=MESH)
    for k in range(1, ctx):
        pl.semaphore_signal(
            barrier, inc=1, device_id={"ctx": lax.rem(z + k, ctx)}, device_id_type=MESH
        )

    gain = 1.0 + scale_ref[...].astype(jnp.float32)
    shift = shift_ref[...].astype(jnp.float32)

    def norm_chunk(c):
        def norm_rows(at, _):
            hid = stream_ref[0, pl.ds(c * part + at * 16, 16), :].astype(jnp.float32)
            mean = jnp.mean(hid, axis=-1, keepdims=True)
            cen = hid - mean
            var = jnp.mean(cen * cen, axis=-1, keepdims=True)
            toks[c, 0, pl.ds(at * 16, 16), :] = (
                cen * lax.rsqrt(var + 1e-06) * gain + shift
            ).astype(jnp.bfloat16)
            return 0

        lax.fori_loop(0, part // 16, norm_rows, 0)

    t_sent = []

    def send_tok(c, role_from, to_mask, role_to, sib, half):
        n = len(t_sent)
        copy = pltpu.make_async_remote_copy(
            src_ref=toks.at[c, role_from, pl.ds(half * piece, piece), :],
            dst_ref=toks.at[c, role_to, pl.ds(sib * part + half * piece, piece), :],
            send_sem=t_send.at[n],
            recv_sem=t_recv.at[c, role_to, sib, half],
            device_id={"dp": flip(i, to_mask)},
            device_id_type=MESH,
        )
        copy.start()
        t_sent.append(copy)

    def wait_tok(c, role, sib, half):
        ref = toks.at[c, role, pl.ds(sib * part + half * piece, piece), :]
        pltpu.make_async_copy(ref, ref, t_recv.at[c, role, sib, half]).wait()

    def pass_on(c, role, half):
        for bit in range(bits):
            to = role ^ (1 << bit)
            if role >> bit & 1:
                continue
            if role == 0 or last_hop(to, half) == bit:
                send_tok(c, role, 2 << bit, to, 0, half)

    def pass_sib(c, role, half):
        send_tok(c, role, 1, role, 1, half)

    def send_direct(c):
        for bit in range(bits):
            for half in range(2):
                send_tok(c, 0, 2 << bit, 1 << bit, 0, half if bit % 2 == 0 else 1 - half)

    qg = qg_ref[...]
    kg = kg_ref[...]
    p_sent = []

    def project(c, role):
        def one(j, _):
            u = m * i + j
            kind = u // (ctx * sub)
            flat = jnp.dot(
                toks[c, role],
                weight[:, pl.ds(pl.multiple_of(j * unit, unit), unit)],
                preferred_element_type=jnp.float32,
            ).astype(jnp.bfloat16)
            head_gain = jnp.where(kind == 0, qg, kg)
            for h in range(unit // HD):
                raw = flat[:, h * HD : (h + 1) * HD]
                val = raw.astype(jnp.float32)
                inv = lax.rsqrt(jnp.mean(val * val, axis=-1, keepdims=True) + 1e-06)
                res = jnp.where(kind < 2, val * inv * head_gain, val).astype(jnp.bfloat16)
                proj[c, 2 * role, j, :, h * HD : (h + 1) * HD] = res[:part]
                proj[c, 2 * role + 1, j, :, h * HD : (h + 1) * HD] = res[part:]
            return 0

        lax.fori_loop(0, m, one, 0)
        for k in range(2):
            q = 2 * role + k
            dst = mine.at[c, pl.ds(m * i, m)]
            if q == 0:
                pltpu.make_async_copy(proj.at[c, 0], dst, m_recv.at[c, i]).start()
            else:
                copy = pltpu.make_async_remote_copy(
                    src_ref=proj.at[c, q],
                    dst_ref=dst,
                    send_sem=p_send.at[c, q],
                    recv_sem=m_recv.at[c, i],
                    device_id={"dp": flip(i, q)},
                    device_id_type=MESH,
                )
                copy.start()
                p_sent.append(copy)

    def z_copy(c, q, j):
        u = m * flip(i, q) + j
        kind = u // (ctx * sub)
        to = (u // sub) % ctx
        h = u % sub
        src = mine.at[c, u]
        dst = heads.at[h, kind, pl.ds(z * rows + c * part, part), :]

        def local():
            return pltpu.make_async_copy(src, dst, r_sem.at[h])

        def remote():
            return pltpu.make_async_remote_copy(
                src_ref=src,
                dst_ref=dst,
                send_sem=z_send.at[c, q * m + j],
                recv_sem=r_sem.at[h],
                device_id={"ctx": to},
                device_id_type=MESH,
            )

        return to, local, remote

    def to_heads(c, role):
        for q in (2 * role, 2 * role + 1):
            src = flip(i, q)
            ref = mine.at[c, pl.ds(m * src, m)]
            pltpu.make_async_copy(ref, ref, m_recv.at[c, src]).wait()
            for j in range(m):
                to, local, remote = z_copy(c, q, j)
                pl.when(to == z)(lambda: local().start())
                pl.when(to != z)(lambda: remote().start())

    def wait_sib(c, role):
        for half in range(2):
            wait_tok(c, role, 1, half)

    norm_chunk(0)
    pl.semaphore_wait(barrier, dp + ctx - 2)
    send_direct(0)
    for c in range(CHUNKS):
        if c:
            norm_chunk(c)
        for half in range(2):
            pass_sib(c, 0, half)
    load.wait()
    for c in range(CHUNKS):
        wait_sib(c, 0)
        project(c, 0)
    for c in range(CHUNKS):
        to_heads(c, 0)
    levels = [[r for r in range(chips) if r.bit_count() == n] for n in range(1, bits + 1)]
    done = []
    for c in range(CHUNKS):
        for at, level in enumerate(levels):
            order = [(r, half) for half in range(2) for r in level]
            if len(level) == 2:
                order = [(level[0], 0), (level[1], 1), (level[0], 1), (level[1], 0)]
            for r, half in order:
                wait_tok(c, r, 0, half)
                pass_on(c, r, half)
                pass_sib(c, r, half)
            if at == 0 and c + 1 < CHUNKS:
                send_direct(c + 1)
            for d in done:
                to_heads(*d)
            done = []
            for r in level:
                wait_sib(c, r)
                project(c, r)
                done.append((c, r))
    for d in done:
        to_heads(*d)

    for h in range(sub):
        pltpu.make_async_copy(heads.at[h], heads.at[h], r_sem.at[h]).wait()

    root = 1.0 / math.sqrt(HD)
    o_sent = []
    for k in list(range(1, ctx)) + [0]:
        t = lax.rem(z + k, ctx)
        at = pl.ds(pl.multiple_of(t * rows, rows), rows)
        for h in range(sub):
            for p in range(unit // HD):
                lanes = slice(p * HD, (p + 1) * HD)
                scores = lax.dot_general(
                    heads[h, 0, at, lanes],
                    heads[h, 1, :, lanes],
                    (((1,), (1,)), ((), ())),
                    preferred_element_type=jnp.float32,
                )
                weights = jnp.exp(scores * root)
                totals = jnp.sum(weights, axis=-1, keepdims=True)
                summed = jnp.dot(
                    weights.astype(jnp.bfloat16),
                    heads[h, 2, :, lanes],
                    preferred_element_type=jnp.float32,
                )
                outs[k, :, pl.ds(h * unit + p * HD, HD)] = (summed / totals).astype(jnp.bfloat16)
        dst = out_ref.at[0, :, pl.ds(pl.multiple_of(z * width, width), width)]
        if k:
            copy = pltpu.make_async_remote_copy(
                src_ref=outs.at[k],
                dst_ref=dst,
                send_sem=o_send.at[k],
                recv_sem=o_recv.at[z],
                device_id={"ctx": t},
                device_id_type=MESH,
            )
            copy.start()
            o_sent.append(copy)
        else:
            pltpu.make_async_copy(outs.at[0], dst, o_recv.at[z]).start()

    for s in range(ctx):
        ref = out_ref.at[0, :, pl.ds(s * width, width)]
        pltpu.make_async_copy(ref, ref, o_recv.at[s]).wait()
    for copy in t_sent + p_sent + o_sent:
        copy.wait_send()
    for c in range(CHUNKS):
        for q in range(dp):
            for j in range(m):
                to, _, remote = z_copy(c, q, j)
                pl.when(to != z)(lambda: remote().wait_send())


def shards(mesh, stream, mod_shift, mod_scale, qkv_weight, q_gain, k_gain):
    dp, ctx = mesh.shape["dp"], mesh.shape["ctx"]
    rows, depth = stream.shape[1:]
    cols = qkv_weight.shape[1]
    part = rows // CHUNKS
    chips = dp // 2
    width = HW // ctx
    unit = math.gcd(cols, width)
    m = cols // unit
    sub = width // unit
    seq = rows * ctx
    dma = pltpu.SemaphoreType.DMA
    vmem = pl.BlockSpec(memory_space=pltpu.VMEM)
    return pl.pallas_call(
        functools.partial(kernel, dp, ctx, unit),
        out_shape=jax.ShapeDtypeStruct((1, rows, HW), jnp.bfloat16),
        in_specs=[vmem, vmem, vmem, pl.BlockSpec(memory_space=pl.ANY), vmem, vmem],
        out_specs=vmem,
        scratch_shapes=[
            pltpu.VMEM((CHUNKS, chips, 2 * part, depth), jnp.bfloat16),
            pltpu.VMEM((depth, cols), jnp.bfloat16),
            pltpu.VMEM((CHUNKS, dp, m, part, unit), jnp.bfloat16),
            pltpu.VMEM((CHUNKS, dp * m, part, unit), jnp.bfloat16),
            pltpu.VMEM((sub, 3, seq, unit), jnp.bfloat16),
            pltpu.VMEM((ctx, rows, width), jnp.bfloat16),
            dma,
            dma((4 * dp * CHUNKS,)),
            dma((CHUNKS, chips, 2, 2)),
            dma((CHUNKS, dp)),
            dma((CHUNKS, dp)),
            dma((CHUNKS, dp * m)),
            dma((sub,)),
            dma((ctx,)),
            dma((ctx,)),
        ],
        compiler_params=pltpu.CompilerParams(
            collective_id=0, has_side_effects=True, vmem_limit_bytes=56 * 1024 * 1024
        ),
    )(stream, mod_shift, mod_scale, qkv_weight, q_gain[None, :], k_gain[None, :])


def solution(mesh):
    placed = (P("dp", "ctx", None), P("dp", None), P("dp", None), P(None, "dp"), P(), P())
    return jax.shard_map(
        functools.partial(shards, mesh),
        mesh=mesh,
        in_specs=placed,
        out_specs=P("dp", "ctx", None),
        check_vma=False,
    )
```

time: 90.6 us -> 82.9 us (0.915); the launches traced: 89.2 us -> 82.5 us
  Pallas kernels: 87.3 us -> 80.6 us
    pallas_call x1, Pallas kernels: 87.3 us -> 80.6 us  [shards(): pl.pallas_call(functools.partial(kernel, dp, ctx, unit), out_shape=jax.Sh...]
where the time goes in v2:
time: 82.9 us; the launch traced here: 82.5 us
  Pallas kernels  80.6 us (97%)
  local copies, waits for them, and re-layouts  1.88 us (2%)
    pallas_call x1, Pallas kernels, shards(): pl.pallas_call(functools.partial(kernel, dp, ctx, unit), out_shape=jax.Sh...  80.6 us
    unnamed x1, local copies, waits for them, and re-layouts  1.88 us

profile of v2, /device:TPU:30, one launch (start us, length us, event | category | flops | bytes accessed | tf_op | source)
XLA Modules:
  0.0 82.5 jit_solution(17884826219582307953)
XLA Ops:
  0.0 80.6 %shard_map.64 = bf16[1,128,2048]{2,1,0:T(8,128)(2,1)} custom-call(bf16[1,128,3072]{2,1,0:T(8,128)(2,1)} %stream_ref.1, bf16[1,3072]{1,0:T(2,128)(2,1)} %shift_ref.1, bf16[1,3072]{1,0:T(2,128)(2,1)} %scale_ref.1, bf16[3072,768]{1,0:T(8,128)(2,1)} %weight_hbm.1, f32[1,128]{1,0:T(1,128)} %bitcast.2, f32[1,128]{1,0:T(1,128)} %bitcast.3), custom_call_target="tpu_custom_call" | custom-call | tf_op jit(solution)/shard_map/pallas_call | solution.py:296
  80.6 1.9 %copy.8 = bf16[1,128,2048]{2,1,0:T(8,128)(2,1)} copy(bf16[1,128,2048]{2,1,0:T(8,128)(2,1)} %shard_map.64) | data formatting | bytes 1048576

commit v3 on v2

--- a/solution.py
+++ b/solution.py
@@ -191,12 +191,11 @@
         for half in range(2):
             wait_tok(c, role, 1, half)
 
-    norm_chunk(0)
+    for c in range(CHUNKS):
+        norm_chunk(c)
     pl.semaphore_wait(barrier, dp + ctx - 2)
     send_direct(0)
     for c in range(CHUNKS):
-        if c:
-            norm_chunk(c)
         for half in range(2):
             pass_sib(c, 0, half)
     load.wait()
@@ -218,13 +217,12 @@
                 pass_sib(c, r, half)
             if at == 0 and c + 1 < CHUNKS:
                 send_direct(c + 1)
-            for d in done:
-                to_heads(*d)
-            done = []
             for r in level:
                 wait_sib(c, r)
                 project(c, r)
-                done.append((c, r))
+            for d in done:
+                to_heads(*d)
+            done = [(c, r) for r in level]
     for d in done:
         to_heads(*d)
 

time: 82.9 us -> 82 us (0.989)
  no operation moved by 1% of the time
where the time goes in v3:
time: 82 us; the launch traced here: 81.9 us
  Pallas kernels  80 us (98%)
  local copies, waits for them, and re-layouts  1.88 us (2%)
    pallas_call x1, Pallas kernels, shards(): pl.pallas_call(functools.partial(kernel, dp, ctx, unit), out_shape=jax.Sh...  80 us
    unnamed x1, local copies, waits for them, and re-layouts  1.88 us

profile of v3, /device:TPU:30, one launch (start us, length us, event | category | flops | bytes accessed | tf_op | source)
XLA Modules:
  0.0 81.9 jit_solution(2421380320932080159)
XLA Ops:
  0.0 80.0 %shard_map.64 = bf16[1,128,2048]{2,1,0:T(8,128)(2,1)} custom-call(bf16[1,128,3072]{2,1,0:T(8,128)(2,1)} %stream_ref.1, bf16[1,3072]{1,0:T(2,128)(2,1)} %shift_ref.1, bf16[1,3072]{1,0:T(2,128)(2,1)} %scale_ref.1, bf16[3072,768]{1,0:T(8,128)(2,1)} %weight_hbm.1, f32[1,128]{1,0:T(1,128)} %bitcast.2, f32[1,128]{1,0:T(1,128)} %bitcast.3), custom_call_target="tpu_custom_call" | custom-call | tf_op jit(solution)/shard_map/pallas_call | solution.py:294
  80.0 1.9 %copy.8 = bf16[1,128,2048]{2,1,0:T(8,128)(2,1)} copy(bf16[1,128,2048]{2,1,0:T(8,128)(2,1)} %shard_map.64) | data formatting | bytes 1048576

commit v4 on v3

--- a/solution.py
+++ b/solution.py
@@ -134,25 +134,28 @@
                 res = jnp.where(kind < 2, val * inv * head_gain, val).astype(jnp.bfloat16)
                 proj[c, 2 * role, j, :, h * HD : (h + 1) * HD] = res[:part]
                 proj[c, 2 * role + 1, j, :, h * HD : (h + 1) * HD] = res[part:]
+            for q in (2 * role, 2 * role + 1):
+                dst = mine.at[c, u]
+                if q == 0:
+                    pltpu.make_async_copy(proj.at[c, 0, j], dst, m_recv.at[c, i]).start()
+                else:
+                    back(q, proj.at[c, q, j], dst).start()
             return 0
 
+        def back(q, src, dst):
+            return pltpu.make_async_remote_copy(
+                src_ref=src,
+                dst_ref=dst,
+                send_sem=p_send.at[c, q],
+                recv_sem=m_recv.at[c, i],
+                device_id={"dp": flip(i, q)},
+                device_id_type=MESH,
+            )
+
         lax.fori_loop(0, m, one, 0)
-        for k in range(2):
-            q = 2 * role + k
-            dst = mine.at[c, pl.ds(m * i, m)]
-            if q == 0:
-                pltpu.make_async_copy(proj.at[c, 0], dst, m_recv.at[c, i]).start()
-            else:
-                copy = pltpu.make_async_remote_copy(
-                    src_ref=proj.at[c, q],
-                    dst_ref=dst,
-                    send_sem=p_send.at[c, q],
-                    recv_sem=m_recv.at[c, i],
-                    device_id={"dp": flip(i, q)},
-                    device_id_type=MESH,
-                )
-                copy.start()
-                p_sent.append(copy)
+        for q in (2 * role, 2 * role + 1):
+            if q:
+                p_sent.append(back(q, proj.at[c, q], mine.at[c, pl.ds(m * i, m)]))
 
     def z_copy(c, q, j):
         u = m * flip(i, q) + j

time: 82 us -> 85.1 us (1.038)
  the two profiles are of different devices: /device:TPU:30 before, /device:TPU:28 now
where the time goes in v4:
time: 85.1 us; the launch traced here: 84.9 us
  Pallas kernels  83 us (98%)
  local copies, waits for them, and re-layouts  1.88 us (2%)
    pallas_call x1, Pallas kernels, shards(): pl.pallas_call(functools.partial(kernel, dp, ctx, unit), out_shape=jax.Sh...  83 us
    unnamed x1, local copies, waits for them, and re-layouts  1.88 us

profile of v4, /device:TPU:28, one launch (start us, length us, event | category | flops | bytes accessed | tf_op | source)
XLA Modules:
  0.0 84.9 jit_solution(9437474406139584997)
XLA Ops:
  0.0 83.0 %shard_map.64 = bf16[1,128,2048]{2,1,0:T(8,128)(2,1)} custom-call(bf16[1,128,3072]{2,1,0:T(8,128)(2,1)} %stream_ref.1, bf16[1,3072]{1,0:T(2,128)(2,1)} %shift_ref.1, bf16[1,3072]{1,0:T(2,128)(2,1)} %scale_ref.1, bf16[3072,768]{1,0:T(8,128)(2,1)} %weight_hbm.1, f32[1,128]{1,0:T(1,128)} %bitcast.2, f32[1,128]{1,0:T(1,128)} %bitcast.3), custom_call_target="tpu_custom_call" | custom-call | tf_op jit(solution)/shard_map/pallas_call | solution.py:297
  83.0 1.9 %copy.8 = bf16[1,128,2048]{2,1,0:T(8,128)(2,1)} copy(bf16[1,128,2048]{2,1,0:T(8,128)(2,1)} %shard_map.64) | data formatting | bytes 1048576
